TPU v7x, 32 devices: a whole 2x2x4 slice. The times are simulated.
32 devices in a mesh: grp: 2 (over core), dp: 16 (over z, y, x).
Axes of the slice: x: 2, y: 2, z: 4, core: 2. Of those that a mesh axis runs over, the one named last changes fastest.
Arguments:
- pixels: bfloat16 [2, 2, 16, 8, 196, 768], P(None, None, 'dp', 'grp'), may hold values from -6 to 6
- counts: int32 [2, 2, 16], P(None, None, 'dp'), may hold values from 4 to 8, as said below
- step_mask: int32 [2, 2, 16, 8], P(None, None, 'dp'), may hold values from 0 to 1, as said below
- owner: int32 [2, 16], P(None, 'dp'), may hold values from 0 to 1
- params: bfloat16 [4123136], P(('grp', 'dp'))
- cotangent: bfloat16 [2, 2, 16, 8, 16, 512], P(None, 'grp', 'dp'), may hold values from -6 to 6
Outputs:
- processed: bfloat16 [2, 2, 16, 8, 16, 512], P(None, 'grp', 'dp')
- pixel_grad: bfloat16 [2, 2, 16, 8, 196, 768], P(None, None, 'dp', 'grp')
- param_grad: float32 [4123136], P(('grp', 'dp'))
Inputs may be any that keep to these rules, and one draw needn't show every extreme that they name: `counts`: some clip has 8 frames in every draw. `step_mask`: in each half of a clip's 8 slots (the first 4 and the last 4) 1 to 2 slots hold 1; the clip with 8 frames has exactly 2 in both halves.
All inputs are finite; a program needn't handle non-finite values.
Results may differ from a plain program's by a relative error of at most 0.015.
Values may be sent and summed in bfloat16 or wider, within the bound.
A program may use at most 192 MiB of HBM per device.

v0:
```python
import math

import jax
import jax.numpy as jnp
from jax import lax
from jax.sharding import PartitionSpec as P

D = 512
HEADS = 8
FFN = 2048
PIN = 768
MEM = 96
READ = 16
HID = 512


def as_sent(shard):

    def short(part):
        return part.astype(jnp.bfloat16) if part.dtype == jnp.float32 else part

    return jax.tree.map(short, shard)


def segments():
    return [
        ("patch_weight", (PIN, D)),
        ("patch_bias", (D,)),
        ("read_gain", (D,)),
        ("read_hidden", (D, HID)),
        ("read_scores", (HID, READ)),
        ("attn_gain", (D,)),
        ("qkv_weight", (D, 3 * D)),
        ("attn_out", (D, D)),
        ("ffn_gain", (D,)),
        ("ffn_in", (D, FFN)),
        ("ffn_out", (FFN, D)),
        ("write_gain", (D,)),
        ("write_hidden", (D, HID)),
        ("write_scores", (HID, MEM)),
    ]


def unpack(flat_params):
    pieces = {}
    offset = 0
    for segment_name, extent in segments():
        length = math.prod(extent)
        pieces[segment_name] = flat_params[offset : offset + length].reshape(extent)
        offset = offset + length
    return pieces


def layer_norm(values, scale_vec):
    average = jnp.mean(values, -1, keepdims=True)
    centered = values - average
    variance = jnp.mean(centered * centered, -1, keepdims=True)
    return centered * lax.rsqrt(variance + 1e-06) * scale_vec


def make_model():

    def value_fwd(v):
        return lax.optimization_barrier(v.astype(jnp.bfloat16)).astype(jnp.float32)

    round_value = jax.custom_vjp(value_fwd)

    def value_keep(v):
        return (value_fwd(v), None)

    def value_pass(kept, grad):
        return (grad,)

    round_value.defvjp(value_keep, value_pass)

    def grad_fwd(v):
        return v

    round_grad = jax.custom_vjp(grad_fwd)

    def grad_keep(v):
        return (v, None)

    def grad_round(kept, grad):
        return (value_fwd(grad),)

    round_grad.defvjp(grad_keep, grad_round)

    def product_fwd(operand_a, operand_b):
        return jnp.matmul(
            operand_a.astype(jnp.bfloat16),
            operand_b.astype(jnp.bfloat16),
            preferred_element_type=jnp.float32,
        )

    paired_product = jax.custom_vjp(product_fwd)

    def product_keep(operand_a, operand_b):
        return (product_fwd(operand_a, operand_b), (operand_a, operand_b))

    def product_back(kept, grad):
        operand_a, operand_b = kept
        grad_low = grad.astype(jnp.bfloat16)
        grad_a = jnp.matmul(
            grad_low,
            jnp.swapaxes(operand_b, -1, -2).astype(jnp.bfloat16),
            preferred_element_type=jnp.float32,
        )
        grad_b = jnp.matmul(
            jnp.swapaxes(operand_a, -1, -2).astype(jnp.bfloat16),
            grad_low,
            preferred_element_type=jnp.float32,
        )
        return (grad_a, grad_b)

    paired_product.defvjp(product_keep, product_back)

    def matmul(operand_a, operand_b):
        if operand_b.ndim == 2:
            leading = operand_a.shape[:-1]
            result_rows = paired_product(operand_a.reshape(-1, operand_a.shape[-1]), operand_b)
            return round_grad(result_rows.reshape(leading + (operand_b.shape[1],)))
        return round_grad(paired_product(operand_a, operand_b))

    def summarize(tokens_in, scale_vec, hidden_weight, score_weight):
        normed = round_value(layer_norm(tokens_in, scale_vec))
        hidden = round_value(jax.nn.gelu(matmul(normed, hidden_weight), approximate=False))
        scores = matmul(hidden, score_weight)
        weights = round_value(jax.nn.softmax(scores, axis=1))
        return matmul(jnp.swapaxes(weights, 1, 2), tokens_in)

    def process(summary, pieces):
        batch_size = summary.shape[0]
        head_size = D // HEADS
        normed = round_value(layer_norm(summary, pieces["attn_gain"]))
        united_qkv = round_value(matmul(normed, pieces["qkv_weight"]))
        split_heads = united_qkv.reshape(batch_size, READ, 3, HEADS, head_size).transpose(
            2, 0, 3, 1, 4
        )
        scores = matmul(split_heads[0], jnp.swapaxes(split_heads[1], 2, 3)) * (
            1.0 / math.sqrt(head_size)
        )
        probabilities = round_value(jax.nn.softmax(scores, axis=-1))
        attended = matmul(probabilities, split_heads[2])
        joined = round_value(attended.transpose(0, 2, 1, 3).reshape(batch_size, READ, D))
        middle = summary + matmul(joined, pieces["attn_out"])
        normed_two = round_value(layer_norm(middle, pieces["ffn_gain"]))
        inner_act = round_value(
            jax.nn.gelu(matmul(normed_two, pieces["ffn_in"]), approximate=False)
        )
        return middle + matmul(inner_act, pieces["ffn_out"])

    def advance(pieces, memory, frame_tokens, valid_flag):
        memory_low = round_value(memory)
        summary = summarize(
            jnp.concatenate([memory_low, frame_tokens], 1),
            pieces["read_gain"],
            pieces["read_hidden"],
            pieces["read_scores"],
        )
        tokens_out = round_value(process(summary, pieces))
        written = summarize(
            jnp.concatenate([memory_low, tokens_out, frame_tokens], 1),
            pieces["write_gain"],
            pieces["write_hidden"],
            pieces["write_scores"],
        )
        keep_mask = valid_flag[:, None, None]
        return (jnp.where(keep_mask > 0.5, written, memory), tokens_out * keep_mask)

    def run_core(flat_params, frames, valid_steps):
        pieces = unpack(flat_params)
        frames = round_grad(frames)
        initial = jnp.zeros((frames.shape[0], MEM, D), jnp.float32)

        def step_fn(memory, inputs):
            return advance(pieces, memory, inputs[0], inputs[1])

        final_memory, outputs = lax.scan(
            jax.checkpoint(step_fn),
            initial,
            (jnp.swapaxes(frames, 0, 1), jnp.swapaxes(valid_steps, 0, 1)),
        )
        return jnp.swapaxes(outputs, 0, 1)

    def stem_forward(flat_params, pixel_block):
        pieces = unpack(flat_params)
        return round_value(matmul(pixel_block, pieces["patch_weight"]) + pieces["patch_bias"])

    return (run_core, stem_forward)


def swap_groups(values, owner_bits):
    flags = (owner_bits == 1).reshape((1, -1) + (1,) * (values.ndim - 2))
    return jnp.where(flags, values[::-1], values)


def body(pixels, counts, step_mask, owner, params, cotangent):
    run_core, stem_forward = make_model()
    micro_count = pixels.shape[0]
    steps_full = cotangent.shape[3]
    core_index = lax.axis_index("grp")
    positions = jnp.arange(steps_full, dtype=jnp.int32)
    valid_all = ((positions < counts[..., None]) & (step_mask == 1)).astype(jnp.float32)
    shard_grad = jnp.zeros(params.shape, jnp.float32)
    processed_list = []
    pixel_list = []
    for micro_index in range(micro_count):
        whole = lax.all_gather(params, ("grp", "dp"), axis=0, tiled=True)
        flat_params = whole.astype(jnp.float32)
        owner_bits = owner[micro_index]
        valid_micro = valid_all[micro_index]
        valid_owned = lax.dynamic_index_in_dim(
            swap_groups(valid_micro, owner_bits), core_index, 0, keepdims=False
        )
        embedded, stem_back = jax.vjp(
            stem_forward, flat_params, pixels[micro_index].astype(jnp.float32)
        )
        embedded_low = embedded.astype(jnp.bfloat16)
        cot_owned = cotangent[micro_index, 0]
        arrived = lax.all_to_all(
            as_sent(swap_groups(embedded_low, owner_bits)),
            "grp",
            split_axis=0,
            concat_axis=2,
            tiled=True,
        )
        tokens_out, core_back = jax.vjp(
            lambda w, f: run_core(w, f, valid_owned), flat_params, arrived[0].astype(jnp.float32)
        )
        grad_core, grad_frames = core_back(cot_owned.astype(jnp.float32))
        returned = lax.all_to_all(
            grad_frames.astype(jnp.bfloat16)[None], "grp", split_axis=2, concat_axis=0, tiled=True
        )
        grad_embedded = swap_groups(returned, owner_bits).astype(jnp.float32)
        grad_stem, grad_pixels = stem_back(grad_embedded)
        grad_micro = grad_core + grad_stem
        shard_grad = shard_grad + lax.psum_scatter(
            grad_micro, ("grp", "dp"), scatter_dimension=0, tiled=True
        )
        processed_list.append(tokens_out.astype(jnp.bfloat16))
        pixel_list.append(grad_pixels.astype(jnp.bfloat16))
    processed = jnp.stack(processed_list, 0)[:, None]
    pixel_grad = jnp.stack(pixel_list, 0)
    return (processed, pixel_grad, shard_grad)


def solution(mesh):
    return jax.shard_map(
        body,
        mesh=mesh,
        in_specs=(
            P(None, None, "dp", "grp", None, None),
            P(None, None, "dp"),
            P(None, None, "dp", None),
            P(None, "dp"),
            P(("grp", "dp")),
            P(None, "grp", "dp", None, None, None),
        ),
        out_specs=(
            P(None, "grp", "dp", None, None, None),
            P(None, None, "dp", "grp", None, None),
            P(("grp", "dp")),
        ),
        check_vma=False,
    )
```

profile of v0, /device:TPU:0, one launch (start us, length us, event | category | flops | bytes accessed | tf_op | source)
XLA Modules:
  0.0 2013.2 jit_solution(10718461739394709211)
XLA Ops:
  7.2 3.6 broadcast.4858
  10.8 4.6 dynamic-update-slice
  16.2 5.5 fusion.549
  25.0 4.1 convert_element_type.2664
  31.1 3.6 copy.147
  34.7 4.2 convert_element_type.2667
  40.3 155.3 %all-reduce.39.cloned.1.call-done = bf16[4123136]{0:T(1024)(128)(2,1)} async-done(((bf16[4123136]{0:T(1024)(128)(2,1)}), bf16[4123136]{0:T(1024)(128)(2,1)}) %all-reduce.39.cloned.1.call-update) | async-done | bytes 8246288
  199.1 3.3 fusion.492
  202.4 2.6 fusion.493
  207.4 4.6 all-to-all-start
  216.4 4.6 fusion.548
  221.0 4.2 reshape.4621
  225.2 4.4 slice.233
  229.6 2.9 slice.274
  232.5 3.3 reshape.4620
  236.9 3.7 copy.116
  242.2 143.4 %while.112 = (s32[]{:T(128)}, bf16[1,96,512]{2,1,0:T(8,128)(2,1)S(1)}, bf16[8,1,16,512]{3,2,1,0:T(8,128)(2,1)}, bf16[8,1,96,512]{3,2,1,0:T(8,128)(2,1)}, f32[8,1...) while((s32[]{:T(128)}, ...), condition=%wide.region_15.16_spmd.clone, body=%wide.region_0.15_spmd.clone.sunk | while | flops 514051360 | bytes 26326164 | solution.py:179
  253.4 2.6 fusion.927
  261.8 2.6 fusion.912
  271.3 2.6 fusion.927
  279.7 2.6 fusion.912
  289.2 2.6 fusion.927
  297.6 2.6 fusion.912
  307.1 2.6 fusion.927
  325.1 2.6 fusion.927
  333.5 2.6 fusion.912
  343.0 2.6 fusion.927
  351.4 2.6 fusion.912
  360.9 2.6 fusion.927
  369.3 2.6 fusion.912
  378.8 2.6 fusion.927
  386.9 502.6 %while.114 = (s32[]{:T(128)}, f32[512]{0:T(512)}, f32[512,512]{1,0:T(8,128)}, f32[512,16]{0,1:T(8,128)}, f32[512]{0:T(512)}, /*index=5*/f32[512,1536]{1,0:T(8,12...) while((s32[]{:T(128)}, f32[512]{0:T(512)}, ...), condition=%wide.region_62.63_spmd.clone, body=%wide.region_32.62_spmd.clone.sunk | while | flops 1476966656 | bytes 236377168 | solution.py:179
  891.0 5.0 all_to_all.42
  900.8 5.0 convolution_bitcast_fusion.13
  905.8 3.0 copy.134
  908.8 3.0 copy.153
  911.8 5.4 copy.149
  917.2 2.8 copy.150
  920.0 4.4 reshape.4628
  924.4 2.6 copy.148
  935.8 5.0 all_to_all.43
  944.6 149.5 %while.113 = (s32[]{:T(128)}, bf16[1,96,512]{2,1,0:T(8,128)(2,1)S(1)}, bf16[8,1,16,512]{3,2,1,0:T(8,128)(2,1)}, bf16[8,1,96,512]{3,2,1,0:T(8,128)(2,1)}, f32[8,1...) while((s32[]{:T(128)}, ...), condition=%wide.region_31.32_spmd.clone, body=%wide.region_16.31_spmd.clone.sunk | while | flops 514051360 | bytes 26326164 | solution.py:179
  955.8 2.6 fusion.965
  974.5 2.6 fusion.965
  993.2 2.6 fusion.965
  1002.3 2.6 fusion.950
  1011.9 2.6 fusion.965
  1021.0 2.6 fusion.950
  1030.6 2.6 fusion.965
  1049.2 2.6 fusion.965
  1067.9 2.6 fusion.965
  1077.1 2.6 fusion.950
  1086.6 2.6 fusion.965
  1095.4 510.0 %while.115 = (s32[]{:T(128)}, f32[512]{0:T(512)}, f32[512,512]{1,0:T(8,128)}, f32[512,16]{0,1:T(8,128)}, f32[512]{0:T(512)}, /*index=5*/f32[512,1536]{1,0:T(8,12...) while((s32[]{:T(128)}, f32[512]{0:T(512)}, ...), condition=%wide.region_93.94_spmd.clone, body=%wide.region_63.93_spmd.clone.sunk | while | flops 1476966656 | bytes 236376848 | solution.py:179
  1607.0 5.0 all_to_all.44
  1614.0 4.9 convolution_bitcast_fusion.12
  1619.0 3.0 copy.137
  1622.0 2.9 copy.159
  1624.9 5.5 copy.155
  1630.4 2.9 copy.156
  1633.4 4.5 reshape.4637
  1642.5 86.4 %add_add_fusion.8 = f32[4123136]{0:T(1024)} fusion(f32[393216]{0:T(1024)} %bitcast.1737, f32[512]{0:T(512)S(1)} %get-tuple-element.2457, f32[512]{0:T(512)S(1)} %copy-done.191, f32[262144]{0:T(1024)} %bitcast.1749, f32[8192]{0:T(1024)S(1)} %reshape.4638, f32[512]{0:T(512)S(1)} %copy-done.194, f32[786432]{0:T(1024)} %reshape.4637, f32[262144]{0:T(1024)} %bitcast.1748, ...), kind=kLoop, calls=%fused_computation.850 | loop fusion | flops 111324672 | bytes 49477632 | tf_op jit(solution)/shard_map/add | solution.py:238
  1734.0 4.1 copy.138
  1738.8 265.3 %all-reduce.41.cloned.1.call-done = f32[4123136]{0:T(1024)} async-done(((f32[4123136]{0:T(1024)}), f32[4123136]{0:T(1024)}) %all-reduce.41.cloned.1.call-update) | async-done | bytes 16492560
  (5490 shorter events, 1258.8 us)
Async XLA Ops:
  7.2 188.4 %all-reduce.39.cloned.1.call-start = ((), (), s32[]{:S(2)}) async-start(), calls=%async_computation.4 | async-start | bytes 16494592
  207.4 29.5 %all-to-all-start = ((bf16[2,1,4,196,512]{4,2,3,1,0:T(4,128)(2,1)}), bf16[2,1,4,196,512]{4,2,3,1,0:T(4,128)(2,1)}, u32[]{:S(2)}, u32[]{:S(2)}) async-start(bf16[2,1,4,196,512]{4,2,3,1,0:T(4,128)(2,1)} %copy.115), calls=%async_computation | async-start | bytes 3211264 | tf_op jit(solution)/shard_map/all_to_all | solution.py:221
  212.0 1792.1 %all-reduce.41.cloned.1.call-start = ((), (), s32[]{:S(2)}) async-start(), calls=%async_computation.5 | async-start | bytes 32989184
  387.3 11.6 copy-start.124
  387.3 14.5 copy-start.120
  387.3 17.7 copy-start.138
  449.2 12.6 copy-start.124
  449.2 15.4 copy-start.120
  449.3 18.6 copy-start.138
  512.1 12.6 copy-start.124
  512.1 15.4 copy-start.120
  512.1 18.6 copy-start.138
  574.9 12.6 copy-start.124
  574.9 15.4 copy-start.120
  574.9 18.6 copy-start.138
  637.7 12.6 copy-start.124
  637.7 15.4 copy-start.120
  637.7 18.6 copy-start.138
  700.8 12.6 copy-start.124
  700.8 15.4 copy-start.120
  700.8 18.6 copy-start.138
  763.6 12.6 copy-start.124
  763.6 15.4 copy-start.120
  763.6 18.6 copy-start.138
  826.5 12.6 copy-start.124
  826.5 15.4 copy-start.120
  826.5 18.6 copy-start.138
  1095.9 12.4 copy-start.126
  1095.9 15.2 copy-start.122
  1095.9 18.5 copy-start.140
  1158.7 11.2 copy-start.144
  1158.7 11.2 copy-start.134
  1158.7 13.3 copy-start.126
  1158.7 16.2 copy-start.122
  1158.7 19.4 copy-start.140
  1222.5 11.2 copy-start.144
  1222.5 11.2 copy-start.134
  1222.5 13.3 copy-start.126
  1222.5 16.2 copy-start.122
  1222.5 19.4 copy-start.140
  1286.3 11.2 copy-start.144
  1286.3 11.2 copy-start.134
  1286.3 13.3 copy-start.126
  1286.3 16.2 copy-start.122
  1286.3 19.4 copy-start.140
  1350.1 11.2 copy-start.144
  1350.1 11.2 copy-start.134
  1350.1 13.3 copy-start.126
  1350.1 16.2 copy-start.122
  1350.1 19.4 copy-start.140
  1413.9 11.2 copy-start.144
  1413.9 11.2 copy-start.134
  1413.9 13.3 copy-start.126
  1413.9 16.2 copy-start.122
  1413.9 19.4 copy-start.140
  1477.7 11.2 copy-start.144
  1477.7 11.2 copy-start.134
  1477.7 13.3 copy-start.126
  1477.7 16.2 copy-start.122
  1477.7 19.4 copy-start.140
  1541.5 11.2 copy-start.144
  1541.5 13.3 copy-start.126
  1541.5 16.2 copy-start.122
  1541.5 19.4 copy-start.140
  (1450 other events, 4828.3 us)
Sparse Core Ops, SparseCore 0:
  15.6 179.9 all-reduce.38
  1729.0 274.9 all-reduce.40
where the time goes:
time: 2040 us; the launch traced here: 2010 us
  matrix products  619 us (30%)
  other arithmetic  476 us (23%)
  local copies, waits for them, and re-layouts  425 us (21%)
  waiting for transfers between devices  421 us (21%)
  loops' own time  37.1 us (2%)
    dot_general x516, matrix products, matmul(): paired_product(operand_a.reshape(-1, operand_a.shape[-1]), operand_b)  539 us
    unnamed x4, waiting for transfers between devices  421 us
    while x2944, local copies, waits for them, and re-layouts  140 us
    add x1, other arithmetic, body(): shard_grad + lax.psum_scatter(grad_micro, ('grp', 'dp'), scatter_dimensio...  86.4 us
    dot_general x208, matrix products, matmul(): return round_grad(paired_product(operand_a, operand_b))  68.5 us
    reduce_sum x64, other arithmetic, layer_norm(): centered = values - average  60.8 us
    convert_element_type x32, other arithmetic, summarize(): round_value(jax.nn.gelu(matmul(normed, hidden_weight), approximate=False))  56.1 us
    unnamed x98, local copies, waits for them, and re-layouts  56.1 us

commit v1 on v0

v1 whole, which is shorter than its diff:
```python
import functools
import math

import jax
import jax.numpy as jnp
from jax import lax
from jax.experimental import pallas as pl
from jax.experimental.pallas import tpu as pltpu
from jax.sharding import PartitionSpec as P

MESH = pl.DeviceIdType.MESH
F32 = jnp.float32
BF16 = jnp.bfloat16

D = 512
HEADS = 8
HEAD = D // HEADS
FFN = 2048
PIN = 768
P_SIZE = 196
ROWS = 208
MEM = 96
READ = 16
NCOL = MEM + READ
STEPS = 8
BLOCK = 16
EPS = 1e-6
RING = 4
HUGE = 1e30

ROW_PATCH = 0
ROW_BIAS = 768
ROW_RGAIN = 769
ROW_RHID = 770
ROW_RSCORE = 1282
ROW_AGAIN = 1298
ROW_QKV = 1299
ROW_AOUT = 2835
ROW_FGAIN = 3347
ROW_FIN = 3348
ROW_FOUT = 5396
ROW_WGAIN = 7444
ROW_WHID = 7445
ROW_WSCORE = 7957
ROW_END = 8053

VMEM_LIMIT = 60 * 2**20


def dot(a, b, ca=1, cb=0):
    return lax.dot_general(a, b, (((ca,), (cb,)), ((), ())), preferred_element_type=F32)


def window_rows(length):
    return (length + BLOCK * D - 2) // (BLOCK * D) * BLOCK + BLOCK


def plan(chips):
    bits = chips.bit_length() - 1
    low = [b for b in (0, 1) if b < bits]
    high = list(range(low[-1] + 1 if low else 0, bits))
    return high + low, high + low[::-1]


def partners(chips, core, me):
    orders = plan(chips)
    steps = []
    for one, two in zip(*orders):
        a = (1 - 2 * ((me // (1 << one)) % 2)) * (1 << one)
        b = (1 - 2 * ((me // (1 << two)) % 2)) * (1 << two)
        steps.append(a + core * (b - a))
    return steps


def shifted(me, steps, r):
    at = me
    for k, step in enumerate(steps):
        if (r >> k) & 1:
            at = at + step
    return at


def first_block(index, length):
    return (index * length) // (BLOCK * D)


def gather_order(chips):
    return sorted(range(1, chips), key=lambda r: (bin(r).count("1"), r))


def greet(core, me, steps):
    barrier = pltpu.get_barrier_semaphore()
    places = [(core, me + step) for step in steps] + [(1 - core, me)]
    for place in places:
        pl.semaphore_signal(barrier, inc=1, device_id=place, device_id_type=MESH)
    pl.semaphore_wait(barrier, len(places))


def gather_kernel(chips, win, pix, out, pixout, send, recv, sibsend, sibrecv, local, pixsem):
    core = lax.axis_index("grp")
    me = lax.axis_index("dp")
    steps = partners(chips, core, me)
    bits = len(steps)
    sibling = (1 - core, me)
    greet(core, me, steps)

    def remote(src, dst, s, r, place):
        return pltpu.make_async_remote_copy(
            src_ref=src, dst_ref=dst, send_sem=s, recv_sem=r, device_id=place, device_id_type=MESH
        )

    mine = core * chips + me
    started = []
    for k in range(bits - 1, -1, -1):
        copy = remote(win, out.at[mine], send.at[k, 0], recv.at[1 << k], (core, me + steps[k]))
        copy.start()
        started.append(copy)
    keep = pltpu.make_async_copy(win, out.at[mine], local.at[0])
    keep.start()
    keep_pix = pltpu.make_async_copy(pix.at[0], pixout.at[core], local.at[1])
    keep_pix.start()
    swap_pix = remote(pix.at[1], pixout.at[core], pixsem.at[0], pixsem.at[1], sibling)
    swap_pix.start()
    side = [remote(win, out.at[mine], sibsend.at[0], sibrecv.at[0], sibling)]
    side[0].start()
    for r in gather_order(chips):
        at = out.at[core * chips + shifted(me, steps, r)]
        top = r.bit_length() - 1
        remote(at, at, send.at[0, 0], recv.at[r], sibling).wait_recv()
        for k in range(bits - 1, top, -1):
            copy = remote(at, at, send.at[k, r], recv.at[r | (1 << k)], (core, me + steps[k]))
            copy.start()
            started.append(copy)
        copy = remote(at, at, sibsend.at[r], sibrecv.at[r], sibling)
        copy.start()
        side.append(copy)
    for copy in started:
        copy.wait_send()
    for copy in side:
        copy.wait()
    keep.wait()
    keep_pix.wait()
    swap_pix.wait()


def gather(win, pix, chips):
    rows = win.shape[0]
    bits = chips.bit_length() - 1
    return pl.pallas_call(
        functools.partial(gather_kernel, chips),
        out_shape=(
            jax.ShapeDtypeStruct((2 * chips, rows, D), BF16),
            jax.ShapeDtypeStruct((2, 4, ROWS, PIN), BF16),
        ),
        in_specs=[pl.BlockSpec(memory_space=pl.ANY)] * 2,
        out_specs=[pl.BlockSpec(memory_space=pl.ANY)] * 2,
        scratch_shapes=[
            pltpu.SemaphoreType.DMA((bits, chips)),
            pltpu.SemaphoreType.DMA((chips,)),
            pltpu.SemaphoreType.DMA((chips,)),
            pltpu.SemaphoreType.DMA((chips,)),
            pltpu.SemaphoreType.DMA((2,)),
            pltpu.SemaphoreType.DMA((2,)),
        ],
        compiler_params=pltpu.CompilerParams(collective_id=0, has_side_effects=True),
        name="gather",
    )(win, pix)


def reduce_kernel(
    chips, length, grads, pg, out, pgout, own, side, held, send, recv, sibsend, sibrecv, local, pixsem
):
    core = lax.axis_index("grp")
    me = lax.axis_index("dp")
    steps = partners(chips, core, me)
    other_steps = partners(chips, 1 - core, me)
    bits = len(steps)
    rows = own.shape[1]
    sibling = (1 - core, me)

    def remote(src, dst, s, r, place):
        return pltpu.make_async_remote_copy(
            src_ref=src, dst_ref=dst, send_sem=s, recv_sem=r, device_id=place, device_id_type=MESH
        )

    def window(index):
        start = pl.multiple_of(first_block(index, length) * BLOCK, BLOCK)
        return grads.at[pl.ds(start, rows)]

    def mine(r):
        src = window(core * chips + shifted(me, steps, r))
        return pltpu.make_async_copy(src, own.at[r], local.at[r])

    for r in range(chips - 1, -1, -1):
        mine(r).start()
    greet(core, me, steps)
    swaps = []
    for r in range(chips - 1, -1, -1):
        src = window((1 - core) * chips + shifted(me, other_steps, r))
        copy = remote(src, side.at[r], sibsend.at[r], sibrecv.at[r], sibling)
        copy.start()
        swaps.append(copy)
    swap_pix = remote(pg.at[1 - core], pgout.at[1], pixsem.at[0], pixsem.at[1], sibling)
    swap_pix.start()
    keep_pix = pltpu.make_async_copy(pg.at[core], pgout.at[0], local.at[chips])
    keep_pix.start()

    started = []
    for r in range(chips - 1, -1, -1):
        mine(r).wait()
        remote(side.at[r], side.at[r], sibsend.at[r], sibrecv.at[r], sibling).wait_recv()
        top = r.bit_length() - 1
        slots = []
        for k in range(bits - 1, top, -1):
            slot = held.at[(1 << k) - 1 + r]
            remote(slot, slot, send.at[r], recv.at[(1 << k) - 1 + r], sibling).wait_recv()
            slots.append((1 << k) - 1 + r)

        def add(i, carry, r=r, slots=tuple(slots)):
            at = pl.ds(pl.multiple_of(i * BLOCK, BLOCK), BLOCK)
            total = own[r, at, :].astype(F32) + side[r, at, :].astype(F32)
            for slot in slots:
                total = total + held[slot, at, :].astype(F32)
            if r == 0:
                out[at, :] = total
            else:
                own[r, at, :] = total.astype(BF16)
            return carry

        lax.fori_loop(0, rows // BLOCK, add, 0)
        if r > 0:
            at = r - (1 << top)
            slot = (1 << top) - 1 + at
            copy = remote(
                own.at[r], held.at[slot], send.at[r], recv.at[slot], (core, me + steps[top])
            )
            copy.start()
            started.append(copy)
    for copy in started:
        copy.wait_send()
    for copy in swaps:
        copy.wait_send()
    swap_pix.wait()
    keep_pix.wait()


def reduce(grads, pg, chips, length):
    rows = window_rows(length)
    return pl.pallas_call(
        functools.partial(reduce_kernel, chips, length),
        out_shape=(
            jax.ShapeDtypeStruct((rows, D), F32),
            jax.ShapeDtypeStruct((2, 4, ROWS, PIN), BF16),
        ),
        in_specs=[pl.BlockSpec(memory_space=pl.ANY)] * 2,
        out_specs=[pl.BlockSpec(memory_space=pltpu.VMEM), pl.BlockSpec(memory_space=pl.ANY)],
        scratch_shapes=[
            pltpu.VMEM((chips, rows, D), BF16),
            pltpu.VMEM((chips, rows, D), BF16),
            pltpu.VMEM((chips - 1, rows, D), BF16),
            pltpu.SemaphoreType.DMA((chips,)),
            pltpu.SemaphoreType.DMA((chips,)),
            pltpu.SemaphoreType.DMA((chips,)),
            pltpu.SemaphoreType.DMA((chips,)),
            pltpu.SemaphoreType.DMA((chips + 1,)),
            pltpu.SemaphoreType.DMA((2,)),
        ],
        compiler_params=pltpu.CompilerParams(
            collective_id=1, has_side_effects=True, vmem_limit_bytes=VMEM_LIMIT
        ),
        name="reduce",
    )(grads, pg)


def pick_kernel(where_ref, pix_ref, out_ref):
    out_ref[0, 0, :P_SIZE] = pix_ref[0, 0, 0, 0]
    out_ref[0, 0, P_SIZE:] = jnp.zeros((ROWS - P_SIZE, PIN), BF16)


def pick(pixels, where):
    def source(e, where_ref):
        return ((e // 2) % 2, where_ref[0, e], 0, where_ref[1, e], 0, 0)

    return pl.pallas_call(
        pick_kernel,
        out_shape=jax.ShapeDtypeStruct((2, 4, ROWS, PIN), BF16),
        grid_spec=pltpu.PrefetchScalarGridSpec(
            num_scalar_prefetch=1,
            grid=(8,),
            in_specs=[pl.BlockSpec((1, 1, 1, 1, P_SIZE, PIN), source)],
            out_specs=pl.BlockSpec((1, 1, ROWS, PIN), lambda e, w: (e // 4, e % 4, 0, 0)),
        ),
        name="pick",
    )(where, pixels)


def place_kernel(where_ref, grad_ref, out_ref):
    e = pl.program_id(0)

    @pl.when(where_ref[1, e] == 1)
    def _():
        out_ref[0, 0, 0, 0] = grad_ref[0, :P_SIZE]

    @pl.when(where_ref[1, e] == 0)
    def _():
        out_ref[0, 0, 0, 0] = jnp.zeros((P_SIZE, PIN), BF16)


def place(grads, where, shape):
    return pl.pallas_call(
        place_kernel,
        out_shape=jax.ShapeDtypeStruct(shape, BF16),
        grid_spec=pltpu.PrefetchScalarGridSpec(
            num_scalar_prefetch=1,
            grid=(16,),
            in_specs=[pl.BlockSpec((1, ROWS, PIN), lambda e, w: (w[0, e], 0, 0))],
            out_specs=pl.BlockSpec(
                (1, 1, 1, 1, P_SIZE, PIN), lambda e, w: (e // 8, (e // 4) % 2, 0, e % 4, 0, 0)
            ),
        ),
        name="place",
    )(where, grads.reshape(8, ROWS, PIN))


def frame_index(clip, step):
    return (step // 2) * 4 + clip * 2 + step % 2


def norm(x):
    mean = jnp.mean(x, -1, keepdims=True)
    centered = x - mean
    r = lax.rsqrt(jnp.mean(centered * centered, -1, keepdims=True) + EPS)
    return centered * r, r


def norm_back(g, xh, r):
    return r * (g - jnp.mean(g, -1, keepdims=True) - xh * jnp.mean(g * xh, -1, keepdims=True))


def gelu(x):
    cdf = 0.5 + 0.5 * lax.erf(x * math.sqrt(0.5))
    slope = cdf + x * (jnp.exp(-0.5 * x * x) * (1.0 / math.sqrt(2.0 * math.pi)))
    return (x * cdf).astype(BF16), slope.astype(BF16)


def col_sum(x):
    return jnp.sum(x, 0, keepdims=True)


def row_sum(x):
    return jnp.sum(x, -1, keepdims=True)


def row_max(x):
    return jnp.max(x, -1, keepdims=True)


def iota(shape, dim):
    return lax.broadcasted_iota(jnp.int32, shape, dim)


def score_masks(width, part):
    group = 512 // math.gcd(512, width)
    lane = iota((D, D), 1) + 512 * part
    hidden = iota((D, D), 0)
    where = ((hidden % group) == (lane // width)).astype(BF16)
    lane = iota((width, D), 1) + 512 * part
    pick = ((lane % width) == iota((width, D), 0)).astype(BF16)
    rows = 512 // group
    spread = ((iota((D, rows), 0) // group) == iota((D, rows), 1)).astype(BF16)
    return where, pick, spread


def main_kernel(
    chips,
    length,
    slot_ref,
    flag_ref,
    shards,
    px,
    cot,
    done,
    pg,
    flat,
    planes,
    wp,
    wr,
    ww,
    wqkv,
    wo,
    win,
    wout,
    wsr,
    wsw,
    gains,
    xs,
    a_r,
    a_w,
    h_r,
    h_w,
    d_r,
    d_w,
    ps,
    rs,
    top,
    tot,
    scale,
    cs,
    dsc,
    mem,
    dmem,
    mls,
    mxh,
    mr,
    mnew,
    al_r,
    al_m,
    al_t,
    zs,
    xh1,
    r1,
    us,
    qs,
    prob,
    att,
    xh2,
    r2,
    u2,
    gs,
    dg,
    toks,
    xhk,
    rk,
    dqs,
    dys,
    dpre,
    dos,
    acc_r,
    acc_w,
    vecs,
    ring,
    ring_sem,
):
    rows = shards.shape[1]
    frames = 8

    def fetch(i):
        return pltpu.make_async_copy(shards.at[i], ring.at[i % RING], ring_sem.at[i % RING])

    def lay(i, carry):
        fetch(i).wait()
        start = pl.multiple_of(first_block(i, length) * BLOCK, BLOCK)
        flat[pl.ds(start, BLOCK), :] = flat[pl.ds(start, BLOCK), :] + ring[i % RING, :BLOCK, :]
        start = pl.multiple_of(start + BLOCK, BLOCK)
        flat[pl.ds(start, rows - BLOCK), :] = ring[i % RING, BLOCK:, :]

        @pl.when(i + RING < 2 * chips)
        def _():
            fetch(i + RING).start()

        return carry

    flat[:BLOCK, :] = jnp.zeros((BLOCK, D), BF16)
    for i in range(RING):
        fetch(i).start()
    lax.fori_loop(0, 2 * chips, lay, 0)

    wp[...] = flat[ROW_PATCH : ROW_PATCH + PIN, :]
    wr[...] = flat[ROW_RHID : ROW_RHID + D, :]
    wo[...] = flat[ROW_AOUT : ROW_AOUT + D, :]
    wout[...] = flat[ROW_FOUT : ROW_FOUT + FFN, :]
    ww[...] = flat[ROW_WHID : ROW_WHID + D, :]
    for k, row in enumerate((ROW_BIAS, ROW_RGAIN, ROW_AGAIN, ROW_FGAIN, ROW_WGAIN)):
        base = row // BLOCK * BLOCK
        gains[k : k + 1, :] = flat[base : base + BLOCK, :].astype(F32)[row - base : row - base + 1, :]
    for row, parts, dst in ((ROW_QKV, 3, wqkv), (ROW_FIN, 4, win)):
        for c in range(4):
            at = slice(c * 128, c * 128 + 128)
            planes[c, : parts * D, :] = flat[row : row + parts * D, at].astype(F32)
            for j in range(parts):
                dst[j, :, at] = planes[c, pl.ds(j, D, stride=parts), :].astype(BF16)
    where, chosen, spread = score_masks(READ, 0)
    wide = dot(spread, flat[ROW_RSCORE : ROW_RSCORE + READ, :]).astype(BF16) * where
    wsr[...] = dot(chosen, wide, 1, 1).astype(BF16)
    total = jnp.zeros((MEM, D), F32)
    for c in range(4):
        at = slice(c * 128, c * 128 + 128)
        planes[c, :MEM, :] = flat[ROW_WSCORE : ROW_WSCORE + MEM, at].astype(F32)
    for part in range(3):
        where, chosen, spread = score_masks(MEM, part)
        these = jnp.concatenate(
            [planes[c, pl.ds(part, 32, stride=3), :] for c in range(4)], -1
        ).astype(BF16)
        wide = dot(spread, these).astype(BF16) * where
        total = total + dot(chosen, wide, 1, 1)
    wsw[...] = total.astype(BF16)

    bias = gains[0:1, :]
    g_read = gains[1:2, :]
    g_attn = gains[2:3, :]
    g_ffn = gains[3:4, :]
    g_write = gains[4:5, :]

    lanes = iota((NCOL, ROWS), 1) < P_SIZE

    def frame_forward(f, carry):
        at = pl.ds(pl.multiple_of(f * ROWS, ROWS), ROWS)
        x = (dot(px[f], wp[...]) + bias).astype(BF16)
        xs[f] = x
        xh, r = norm(x.astype(F32))
        a_r[at, :] = (xh * g_read).astype(BF16)
        a_w[at, :] = (xh * g_write).astype(BF16)
        h, d = gelu(dot(a_r[at, :], wr[...]))
        h_r[at, :] = h
        d_r[at, :] = d
        s_read = dot(wsr[...], h, 1, 1)
        h, d = gelu(dot(a_w[at, :], ww[...]))
        h_w[at, :] = h
        d_w[at, :] = d
        s_write = dot(wsw[...], h, 1, 1)
        scores = jnp.where(lanes, jnp.concatenate([s_write, s_read], 0), -HUGE)
        best = row_max(scores)
        p = jnp.exp(scores - best)
        pb = p.astype(BF16)
        ps[f] = pb
        top[f] = best
        tot[f] = row_sum(p)
        rs[f] = dot(pb, x)
        return carry

    lax.fori_loop(0, frames, frame_forward, 0)

    done[...] = jnp.zeros(done.shape, BF16)
    mem[...] = jnp.zeros(mem.shape, F32)
    head_of = [(iota((1, D), 1) // HEAD == h) for h in range(HEADS)]
    same_clip = ((iota((HEADS * 32, 32), 0) // READ) % 2) == (iota((HEADS * 32, 32), 1) // READ)
    zero = jnp.zeros((), F32)

    def by_head(x):
        return jnp.concatenate([jnp.where(m, x, jnp.zeros_like(x)) for m in head_of], 0)

    def from_heads(x):
        total = jnp.where(head_of[0], x[:32], zero)
        for h in range(1, HEADS):
            total = total + jnp.where(head_of[h], x[32 * h : 32 * h + 32], zero)
        return total

    base_r = frames * ROWS
    base_w = frames * ROWS
    base_k = base_w + 2 * 192

    def step_forward(t):
        live = t > 0
        last = t == 3
        if live:
            ml = mem[...].astype(BF16)
            mls[t] = ml
            xh, r = norm(ml.astype(F32))
            mxh[t] = xh
            mr[t] = r
            at = slice(base_r + (t - 1) * 192, base_r + t * 192)
            a = (xh * g_read).astype(BF16)
            a_r[at, :] = a
            h, d = gelu(dot(a, wr[...]))
            h_r[at, :] = h
            d_r[at, :] = d
            if not last:
                a = (xh * g_write).astype(BF16)
                a_w[at, :] = a
                hw, d = gelu(dot(a, ww[...]))
                h_w[at, :] = hw
                d_w[at, :] = d
        z_parts = []
        for b in range(2):
            f = frame_index(b, t)
            m_f = top[f, MEM:, :]
            if live:
                s = dot(wsr[...], h[96 * b : 96 * b + 96], 1, 1)
                best = jnp.maximum(row_max(s), m_f)
                e = jnp.exp(s - best)
                part = row_sum(e)
            else:
                best = jnp.maximum(m_f, 0.0)
                part = MEM * jnp.exp(-best)
            w = jnp.exp(m_f - best)
            inv = 1.0 / (part + w * tot[f, MEM:, :])
            scale[f, MEM:, :] = w * inv
            z = (w * inv) * rs[f, MEM:, :]
            if live:
                al = (e * inv).astype(BF16)
                al_r[t, b] = al
                z = z + dot(al, ml[96 * b : 96 * b + 96])
            z_parts.append(z)
        z = jnp.concatenate(z_parts, 0)
        zs[t] = z
        at = slice(32 * t, 32 * t + 32)
        xh, r = norm(z)
        xh1[t] = xh
        r1[t] = r
        u = (xh * g_attn).astype(BF16)
        us[at, :] = u
        q = dot(u, wqkv[0]).astype(BF16)
        k = dot(u, wqkv[1]).astype(BF16)
        v = dot(u, wqkv[2]).astype(BF16)
        qs[0, t] = q
        qs[1, t] = k
        qs[2, t] = v
        s = jnp.where(same_clip, dot(by_head(q), k, 1, 1) * (1.0 / math.sqrt(HEAD)), -HUGE)
        e = jnp.exp(s - row_max(s))
        p = (e / row_sum(e)).astype(BF16)
        prob[t] = p
        joined = from_heads(dot(p, v)).astype(BF16)
        att[at, :] = joined
        y = z + dot(joined, wo[...])
        xh, r = norm(y)
        xh2[t] = xh
        r2[t] = r
        n = (xh * g_ffn).astype(BF16)
        u2[at, :] = n
        o = y
        for j in range(4):
            g, d = gelu(dot(n, win[j]))
            gs[at, D * j : D * j + D] = g
            dg[t, :, D * j : D * j + D] = d
            o = o + dot(g, wout[D * j : D * j + D, :])
        tok = o.astype(BF16)
        for b in range(2):

            @pl.when(flag_ref[b, t] == 1)
            def _(b=b):
                done[b, slot_ref[b, t]] = tok[16 * b : 16 * b + 16]

        if last:
            return
        toks[t] = tok
        xh, r = norm(tok.astype(F32))
        xhk[t] = xh
        rk[t] = r
        a = (xh * g_write).astype(BF16)
        at = slice(base_k + 32 * t, base_k + 32 * t + 32)
        a_w[at, :] = a
        hk, d = gelu(dot(a, ww[...]))
        h_w[at, :] = hk
        d_w[at, :] = d
        for b in range(2):
            f = frame_index(b, t)
            m_f = top[f, :MEM, :]
            s_tok = dot(wsw[...], hk[16 * b : 16 * b + 16], 1, 1)
            best = jnp.maximum(row_max(s_tok), m_f)
            if live:
                s = dot(wsw[...], hw[96 * b : 96 * b + 96], 1, 1)
                best = jnp.maximum(best, row_max(s))
                e = jnp.exp(s - best)
                part = row_sum(e)
            else:
                best = jnp.maximum(best, 0.0)
                part = MEM * jnp.exp(-best)
            e_tok = jnp.exp(s_tok - best)
            w = jnp.exp(m_f - best)
            inv = 1.0 / (part + row_sum(e_tok) + w * tot[f, :MEM, :])
            scale[f, :MEM, :] = w * inv
            al = (e_tok * inv).astype(BF16)
            al_t[t, b] = al
            new = (w * inv) * rs[f, :MEM, :] + dot(al, tok[16 * b : 16 * b + 16])
            if live:
                al = (e * inv).astype(BF16)
                al_m[t, b] = al
                new = new + dot(al, ml[96 * b : 96 * b + 96])
            mnew[t, b] = new
            old = mem[96 * b : 96 * b + 96, :]
            mem[96 * b : 96 * b + 96, :] = jnp.where(flag_ref[b, t] == 1, new, old)

    for t in range(4):
        step_forward(t)

    vecs[...] = jnp.zeros(vecs.shape, F32)
    acc_r[...] = jnp.zeros(acc_r.shape, F32)
    acc_w[...] = jnp.zeros(acc_w.shape, F32)
    dmem[...] = jnp.zeros(dmem.shape, F32)

    def add_vec(k, x):
        vecs[k : k + 1, :] = vecs[k : k + 1, :] + x

    def step_backward(t):
        live = t > 0
        last = t == 3
        gates = [(flag_ref[b, t] == 1).astype(F32) for b in range(2)]
        d_out = [cot[b, slot_ref[b, t]].astype(F32) * gates[b] for b in range(2)]
        d_ml = []
        dh_mem = []
        keeps = []
        if last:
            for b in range(2):
                f = frame_index(b, t)
                dsc[f, :MEM, :] = jnp.zeros((MEM, D), BF16)
                scale[f, :MEM, :] = jnp.zeros((MEM, 1), F32)
                cs[f, :MEM, :] = jnp.zeros((MEM, 1), F32)
                keeps.append(jnp.zeros((96, D), F32))
                d_ml.append(keeps[b])
        else:
            dh_tok = []
            at_k = slice(base_k + 32 * t, base_k + 32 * t + 32)
            hk = h_w[at_k, :]
            tok = toks[t]
            for b in range(2):
                f = frame_index(b, t)
                down = dmem[96 * b : 96 * b + 96, :]
                ds = (down * gates[b]).astype(BF16)
                keeps.append(down * (1.0 - gates[b]))
                dsc[f, :MEM, :] = ds
                c = row_sum(ds.astype(F32) * mnew[t, b])
                cs[f, :MEM, :] = c
                al = al_t[t, b]
                rows_b = slice(16 * b, 16 * b + 16)
                d_out[b] = d_out[b] + dot(al, ds, 0, 0)
                back = (al.astype(F32) * (dot(ds, tok[rows_b], 1, 1) - c)).astype(BF16)
                dh_tok.append(dot(back, wsw[...], 0, 0))
                acc = dot(back, hk[rows_b])
                if live:
                    rows_b = slice(96 * b, 96 * b + 96)
                    ml = mls[t, rows_b, :]
                    al = al_m[t, b]
                    d_ml.append(dot(al, ds, 0, 0))
                    back = (al.astype(F32) * (dot(ds, ml, 1, 1) - c)).astype(BF16)
                    dh_mem.append(dot(back, wsw[...], 0, 0))
                    at = slice(base_w + (t - 1) * 192 + 96 * b, base_w + (t - 1) * 192 + 96 * b + 96)
                    acc = acc + dot(back, h_w[at, :])
                acc_w[...] = acc_w[...] + acc
            dgk = (jnp.concatenate(dh_tok, 0) * d_w[at_k, :].astype(F32)).astype(BF16)
            d_w[at_k, :] = dgk
            da = dot(dgk, ww[...], 1, 1)
            xh = xhk[t]
            add_vec(4, col_sum(da * xh))
            dx = norm_back(da * g_write, xh, rk[t])
            for b in range(2):
                d_out[b] = d_out[b] + dx[16 * b : 16 * b + 16]
        at = slice(32 * t, 32 * t + 32)
        do = jnp.concatenate(d_out, 0)
        dob = do.astype(BF16)
        dos[at, :] = dob
        dn = jnp.zeros((32, D), F32)
        for j in range(4):
            sl = slice(D * j, D * j + D)
            dp = (dot(dob, wout[sl, :], 1, 1) * dg[t, :, sl].astype(F32)).astype(BF16)
            dpre[at, sl] = dp
            dn = dn + dot(dp, win[j], 1, 1)
        add_vec(3, col_sum(dn * xh2[t]))
        dy = do + norm_back(dn * g_ffn, xh2[t], r2[t])
        dyb = dy.astype(BF16)
        dys[at, :] = dyb
        dbig = by_head(dot(dyb, wo[...], 1, 1).astype(BF16))
        p = prob[t]
        q, k, v = qs[0, t], qs[1, t], qs[2, t]
        dp = dot(dbig, v, 1, 1)
        pf = p.astype(F32)
        ds = (pf * (dp - row_sum(dp * pf)) * (1.0 / math.sqrt(HEAD))).astype(BF16)
        dv = dot(p, dbig, 0, 0).astype(BF16)
        dq = from_heads(dot(ds, k)).astype(BF16)
        dk = dot(ds, by_head(q), 0, 0).astype(BF16)
        dqs[0, at, :] = dq
        dqs[1, at, :] = dk
        dqs[2, at, :] = dv
        du = dot(dq, wqkv[0], 1, 1) + dot(dk, wqkv[1], 1, 1) + dot(dv, wqkv[2], 1, 1)
        add_vec(2, col_sum(du * xh1[t]))
        dz = dy + norm_back(du * g_attn, xh1[t], r1[t])
        dzb = dz.astype(BF16)
        c_all = row_sum(dzb.astype(F32) * zs[t])
        dh_r = []
        for b in range(2):
            f = frame_index(b, t)
            ds = dzb[16 * b : 16 * b + 16]
            c = c_all[16 * b : 16 * b + 16]
            dsc[f, MEM:, :] = ds
            cs[f, MEM:, :] = c
            if live:
                rows_b = slice(96 * b, 96 * b + 96)
                al = al_r[t, b]
                d_ml[b] = d_ml[b] + dot(al, ds, 0, 0)
                back = (al.astype(F32) * (dot(ds, mls[t, rows_b, :], 1, 1) - c)).astype(BF16)
                dh_r.append(dot(back, wsr[...], 0, 0))
                at_b = slice(base_r + (t - 1) * 192 + 96 * b, base_r + (t - 1) * 192 + 96 * b + 96)
                acc_r[...] = acc_r[...] + dot(back, h_r[at_b, :])
        if not live:
            return
        at_m = slice(base_r + (t - 1) * 192, base_r + t * 192)
        xh = mxh[t]
        dgr = (jnp.concatenate(dh_r, 0) * d_r[at_m, :].astype(F32)).astype(BF16)
        d_r[at_m, :] = dgr
        da = dot(dgr, wr[...], 1, 1)
        add_vec(1, col_sum(da * xh))
        g = da * g_read
        if not last:
            dgw = (jnp.concatenate(dh_mem, 0) * d_w[at_m, :].astype(F32)).astype(BF16)
            d_w[at_m, :] = dgw
            da = dot(dgw, ww[...], 1, 1)
            add_vec(4, col_sum(da * xh))
            g = g + da * g_write
        dx = norm_back(g, xh, mr[t])
        for b in range(2):
            rows_b = slice(96 * b, 96 * b + 96)
            dmem[rows_b, :] = keeps[b] + d_ml[b] + dx[rows_b]

    for t in range(3, -1, -1):
        step_backward(t)

    def frame_backward(f, carry):
        at = pl.ds(pl.multiple_of(f * ROWS, ROWS), ROWS)
        x = xs[f]
        ds = dsc[f]
        al = ps[f].astype(F32) * scale[f]
        alb = al.astype(BF16)
        back = (al * (dot(ds, x, 1, 1) - cs[f])).astype(BF16)
        acc_w[...] = acc_w[...] + dot(back[:MEM], h_w[at, :])
        acc_r[...] = acc_r[...] + dot(back[MEM:], h_r[at, :])
        xh, r = norm(x.astype(F32))
        dgr = (dot(back[MEM:], wsr[...], 0, 0) * d_r[at, :].astype(F32)).astype(BF16)
        d_r[at, :] = dgr
        da = dot(dgr, wr[...], 1, 1)
        add_vec(1, col_sum(da * xh))
        g = da * g_read
        dgw = (dot(back[:MEM], wsw[...], 0, 0) * d_w[at, :].astype(F32)).astype(BF16)
        d_w[at, :] = dgw
        da = dot(dgw, ww[...], 1, 1)
        add_vec(4, col_sum(da * xh))
        g = g + da * g_write
        dx = (dot(alb, ds, 0, 0) + norm_back(g, xh, r)).astype(BF16)
        a_dx = pl.ds(pl.multiple_of(f * ROWS, ROWS), ROWS)
        xs[f] = dx
        add_vec(0, col_sum(dx.astype(F32)))
        pg[f] = dot(dx, wp[...], 1, 1).astype(BF16)
        return carry

    lax.fori_loop(0, frames, frame_backward, 0)

    n = frames * ROWS
    flat[ROW_PATCH : ROW_PATCH + PIN, :] = dot(
        px[...].reshape(n, PIN), xs[...].reshape(n, D), 0, 0
    ).astype(BF16)
    flat[ROW_RHID : ROW_RHID + D, :] = dot(a_r[...], d_r[...], 0, 0).astype(BF16)
    flat[ROW_WHID : ROW_WHID + D, :] = dot(a_w[...], d_w[...], 0, 0).astype(BF16)
    flat[ROW_AOUT : ROW_AOUT + D, :] = dot(att[...], dys[...], 0, 0).astype(BF16)
    for j in range(4):
        sl = slice(D * j, D * j + D)
        flat[ROW_FOUT + D * j : ROW_FOUT + D * j + D, :] = dot(gs[:, sl], dos[...], 0, 0).astype(BF16)
    for j in range(3):
        part = dot(us[...], dqs[j], 0, 0)
        for c in range(4):
            planes[c, pl.ds(j, D, stride=3), :] = part[:, 128 * c : 128 * c + 128]
    for c in range(4):
        at = slice(128 * c, 128 * c + 128)
        flat[ROW_QKV : ROW_QKV + 3 * D, at] = planes[c, : 3 * D, :].astype(BF16)
    for j in range(4):
        part = dot(u2[...], dpre[:, D * j : D * j + D], 0, 0)
        for c in range(4):
            planes[c, pl.ds(j, D, stride=4), :] = part[:, 128 * c : 128 * c + 128]
    for c in range(4):
        at = slice(128 * c, 128 * c + 128)
        flat[ROW_FIN : ROW_FIN + FFN, at] = planes[c, :FFN, :].astype(BF16)
    where, chosen, spread = score_masks(READ, 0)
    wide = dot(acc_r[...].astype(BF16), chosen, 0, 0).astype(BF16) * where
    flat[ROW_RSCORE : ROW_RSCORE + READ, :] = dot(spread, wide, 0, 0).astype(BF16)
    for part in range(3):
        where, chosen, spread = score_masks(MEM, part)
        wide = dot(acc_w[...].astype(BF16), chosen, 0, 0).astype(BF16) * where
        these = dot(spread, wide, 0, 0)
        for c in range(4):
            planes[c, pl.ds(part, 32, stride=3), :] = these[:, 128 * c : 128 * c + 128]
    for c in range(4):
        at = slice(128 * c, 128 * c + 128)
        flat[ROW_WSCORE : ROW_WSCORE + MEM, at] = planes[c, :MEM, :].astype(BF16)
    for k, row in enumerate((ROW_BIAS, ROW_RGAIN, ROW_AGAIN, ROW_FGAIN, ROW_WGAIN)):
        flat[row : row + 1, :] = vecs[k : k + 1, :].astype(BF16)
    flat[ROW_END:, :] = jnp.zeros((flat.shape[0] - ROW_END, D), BF16)


def main(shards, px, cot, slots, flags, chips, length):
    rows = shards.shape[1]
    total = (2 * chips - 1) * length // (BLOCK * D) * BLOCK + rows
    n = 8 * ROWS
    vmem = pl.BlockSpec(memory_space=pltpu.VMEM)
    smem = pl.BlockSpec(memory_space=pltpu.SMEM)
    v = pltpu.VMEM
    return pl.pallas_call(
        functools.partial(main_kernel, chips, length),
        out_shape=(
            jax.ShapeDtypeStruct((2, STEPS, READ, D), BF16),
            jax.ShapeDtypeStruct((8, ROWS, PIN), BF16),
            jax.ShapeDtypeStruct((total, D), BF16),
        ),
        in_specs=[smem, smem, pl.BlockSpec(memory_space=pl.ANY), vmem, vmem],
        out_specs=[vmem, vmem, vmem],
        scratch_shapes=[
            v((4, FFN, 128), F32),
            v((PIN, D), BF16),
            v((D, D), BF16),
            v((D, D), BF16),
            v((3, D, D), BF16),
            v((D, D), BF16),
            v((4, D, D), BF16),
            v((FFN, D), BF16),
            v((READ, D), BF16),
            v((MEM, D), BF16),
            v((8, D), F32),
            v((8, ROWS, D), BF16),
            v((n + 576, D), BF16),
            v((n + 480, D), BF16),
            v((n + 576, D), BF16),
            v((n + 480, D), BF16),
            v((n + 576, D), BF16),
            v((n + 480, D), BF16),
            v((8, NCOL, ROWS), BF16),
            v((8, NCOL, D), F32),
            v((8, NCOL, 1), F32),
            v((8, NCOL, 1), F32),
            v((8, NCOL, 1), F32),
            v((8, NCOL, 1), F32),
            v((8, NCOL, D), BF16),
            v((192, D), F32),
            v((192, D), F32),
            v((4, 192, D), BF16),
            v((4, 192, D), F32),
            v((4, 192, 1), F32),
            v((3, 2, MEM, D), F32),
            v((4, 2, READ, MEM), BF16),
            v((3, 2, MEM, MEM), BF16),
            v((3, 2, MEM, READ), BF16),
            v((4, 32, D), F32),
            v((4, 32, D), F32),
            v((4, 32, 1), F32),
            v((128, D), BF16),
            v((3, 4, 32, D), BF16),
            v((4, HEADS * 32, 32), BF16),
            v((128, D), BF16),
            v((4, 32, D), F32),
            v((4, 32, 1), F32),
            v((128, D), BF16),
            v((128, FFN), BF16),
            v((4, 32, FFN), BF16),
            v((3, 32, D), BF16),
            v((3, 32, D), F32),
            v((3, 32, 1), F32),
            v((3, 128, D), BF16),
            v((128, D), BF16),
            v((128, FFN), BF16),
            v((128, D), BF16),
            v((READ, D), F32),
            v((MEM, D), F32),
            v((8, D), F32),
            v((RING, rows, D), BF16),
            pltpu.SemaphoreType.DMA((RING,)),
        ],
        compiler_params=pltpu.CompilerParams(vmem_limit_bytes=VMEM_LIMIT),
        name="model",
    )(slots, flags, shards, px, cot)


def body(pixels, counts, step_mask, owner, params, cotangent):
    chips = lax.axis_size("dp")
    length = params.shape[0]
    core = lax.axis_index("grp").astype(jnp.int32)
    dp = lax.axis_index("dp").astype(jnp.int32)
    half = STEPS // 2

    positions = jnp.arange(STEPS, dtype=jnp.int32)
    valid = ((positions < counts[..., None]) & (step_mask == 1)).astype(jnp.int32)
    valid = valid.reshape(2, 2, 2, half)
    number = jnp.sum(valid, -1)
    local = jnp.arange(half, dtype=jnp.int32)
    first = jnp.min(jnp.where(valid == 1, local, half), -1) % half
    second = jnp.maximum(jnp.max(jnp.where(valid == 1, local, -1), -1), 0)
    slot = jnp.stack([first, second], -1)
    flag = jnp.stack([(number > 0), (number > 1)], -1).astype(jnp.int32)
    mine = (core + owner[:, 0]) % 2
    is_mine = jnp.arange(2, dtype=jnp.int32)[None, :] == mine[:, None]

    def of_group(values, groups):
        pick_second = (groups == 1).reshape((2,) + (1,) * (values.ndim - 2))
        return jnp.where(pick_second, values[:, 1], values[:, 0])

    own_slot = of_group(slot, mine)
    own_flag = of_group(flag, mine)
    slots = (own_slot + half * jnp.arange(2, dtype=jnp.int32)[None, :, None]).reshape(2, 4)
    flags = own_flag.reshape(2, 4)

    def of_half(values):
        return jnp.where(core == 1, values[..., 1, :], values[..., 0, :])

    here = of_half(slot)
    here_flag = of_half(flag)
    groups = jnp.stack([mine, 1 - mine], 0)
    picked = jnp.stack([of_group(here, mine), of_group(here, 1 - mine)], 0)
    where_in = jnp.stack(
        [jnp.broadcast_to(groups[:, :, None], (2, 2, 2)).reshape(8), picked.reshape(8)], 0
    )
    hit0 = (here[..., 0:1] == local) & (here_flag[..., 0:1] == 1)
    hit1 = (here[..., 1:2] == local) & (here_flag[..., 1:2] == 1)
    source = (
        jnp.where(is_mine, 0, 4)[:, :, None]
        + 2 * jnp.arange(2, dtype=jnp.int32)[:, None, None]
        + jnp.where(hit0, 0, 1)
    )
    where_out = jnp.stack([source.reshape(16), (hit0 | hit1).astype(jnp.int32).reshape(16)], 0)

    rows = window_rows(length)
    index = core * chips + dp
    offset = (index * length) % (BLOCK * D)
    win = lax.dynamic_update_slice(jnp.zeros((rows * D,), BF16), params, (offset,))
    win = win.reshape(rows, D)

    pix = pick(pixels, where_in)
    shards, px = gather(win, pix, chips)
    cot = cotangent[:, 0, 0]
    done, pg, grads = main(shards, px.reshape(8, ROWS, PIN), cot, slots, flags, chips, length)
    total, pgs = reduce(grads, pg.reshape(2, 4, ROWS, PIN), chips, length)
    shard_grad = lax.dynamic_slice(total.reshape(rows * D), (offset,), (length,))
    pixel_grad = place(pgs, where_out, pixels.shape)
    return (done[:, None, None], pixel_grad, shard_grad)


def solution(mesh):
    return jax.shard_map(
        body,
        mesh=mesh,
        in_specs=(
            P(None, None, "dp", "grp", None, None),
            P(None, None, "dp"),
            P(None, None, "dp", None),
            P(None, "dp"),
            P(("grp", "dp")),
            P(None, "grp", "dp", None, None, None),
        ),
        out_specs=(
            P(None, "grp", "dp", None, None, None),
            P(None, None, "dp", "grp", None, None),
            P(("grp", "dp")),
        ),
        check_vma=False,
    )
```

time: 2040 us -> 245 us (0.12); the launches traced: 2010 us -> 244 us
  matrix products: 619 us -> 0 us
  other arithmetic: 476 us -> 5.49 us
  waiting for transfers between devices: 421 us -> 0 us
  local copies, waits for them, and re-layouts: 425 us -> 20.8 us
  Pallas kernels: 0 us -> 217 us
  loops' own time: 37.1 us -> 0 us
    dot_general x726 -> x0, matrix products: 614 us -> none  [the longest x516 539 us: matmul(): paired_product(operand_a.reshape(-1, operand_a.shape[-1]), operand_b)]
    unnamed x4 -> x0, waiting for transfers between devices: 421 us -> none
    pallas_call x0 -> x5, Pallas kernels: none -> 217 us  [the longest x1 85.9 us: main(): pl.pallas_call(functools.partial(main_kernel, chips, length), out_shape=(...]
    convert_element_type x434 -> x2, other arithmetic: 152 us -> 0.08 us  [the longest x1 0.08 us: body(): (hit0 | hit1).astype(jnp.int32).reshape(16)]
    while x2948 -> x0, local copies, waits for them, and re-layouts: 141 us -> none
    reduce_sum x322 -> x1, other arithmetic: 113 us -> 0.29 us  [body(): number = jnp.sum(valid, -1)]
    add x1 -> x2, other arithmetic: 86.4 us -> 0.15 us  [body(): jnp.where(is_mine, 0, 4)[:, :, None]]
    convert_element_type x106 -> x1, local copies, waits for them, and re-layouts: 62.1 us -> 0.09 us  [body(): (hit0 | hit1).astype(jnp.int32).reshape(16)]
where the time goes in v1:
time: 245 us; the launch traced here: 244 us
  Pallas kernels  217 us (89%)
  local copies, waits for them, and re-layouts  20.8 us (8%)
  other arithmetic  5.49 us (2%)
    pallas_call x1, Pallas kernels, main(): pl.pallas_call(functools.partial(main_kernel, chips, length), out_shape=(...  85.9 us
    pallas_call x1, Pallas kernels, reduce(): pl.pallas_call(functools.partial(reduce_kernel, chips, length), out_shape...  59.5 us
    pallas_call x1, Pallas kernels, gather(): pl.pallas_call(functools.partial(gather_kernel, chips), out_shape=(jax.Sh...  53.8 us
    unnamed x3, local copies, waits for them, and re-layouts  12.9 us
    pallas_call x1, Pallas kernels, place(): pl.pallas_call(place_kernel, out_shape=jax.ShapeDtypeStruct(shape, BF16),...  11.1 us
    pallas_call x1, Pallas kernels, pick(): pl.pallas_call(pick_kernel, out_shape=jax.ShapeDtypeStruct((2, 4, ROWS, P...  6.16 us

profile of v1, /device:TPU:0, one launch (start us, length us, event | category | flops | bytes accessed | tf_op | source)
XLA Modules:
  0.0 243.6 jit_solution(5849103818764353157)
XLA Ops:
  0.6 0.7 fusion.7
  1.3 0.1 add.131
  1.4 0.1 add.132
  1.5 0.7 broadcast_subtract_fusion
  2.2 0.7 compare_bitcast_fusion.3
  2.8 0.1 fusion.6
  2.9 0.1 broadcast_in_dim.85
  3.0 0.1 stack_reshape.8
  3.1 0.8 fusion.5
  3.9 0.1 reshape.462
  3.9 0.3 fusion.11
  4.3 0.1 copy.19
  4.4 0.1 squeeze.29
  4.5 0.1 copy.18
  4.6 0.1 squeeze.28
  4.7 0.1 fusion.1
  4.7 0.1 copy.22
  4.9 0.1 copy.21
  5.0 0.1 squeeze.31
  5.1 0.1 copy.20
  5.1 0.1 squeeze.30
  5.2 0.6 broadcast_select_fusion.2
  5.8 0.1 copy.24
  6.0 0.2 compare_reduce_fusion.1
  6.2 0.1 broadcast_select_fusion.1
  6.3 0.1 stack_reshape.9
  6.4 0.6 pad_add_fusion.3.where_ref
  6.9 0.2 slice_reduce_fusion.1
  7.1 0.1 or_convert_fusion
  7.2 0.1 reshape.463
  7.3 0.1 select_add_fusion
  7.4 0.1 add.145
  7.5 0.6 pad_add_fusion.4.where_ref
  8.1 4.2 %dynamic_update_slice.3 = bf16[139264]{0:T(1024)(128)(2,1)S(1)} dynamic-update-slice(bf16[139264]{0:T(1024)(128)(2,1)S(1)} %broadcast_in_dim.84, bf16[128848]{0:T(1024)(128)(2,1)} %param.10, s32[]{:T(128)S(6)} %select_n.144) | dynamic-update-slice | bytes 515396 | tf_op jit(solution)/shard_map/dynamic_update_slice | solution.py:1007
  12.3 0.9 reshape.456.win
  13.2 5.2 %copy.23.pix_ref = bf16[2,2,1,4,196,768]{5,4,3,2,1,0:T(8,128)(2,1)} copy(bf16[2,2,1,4,196,768]{5,3,4,2,1,0:T(4,128)(2,1)} %param.6) | data formatting | bytes 9633792 | tf_op args[0]
  18.3 6.2 %pick.1.pix = bf16[2,4,208,768]{3,2,1,0:T(8,128)(2,1)} custom-call(s32[2,8]{1,0:T(2,128)} %pad_add_fusion.3.where_ref, bf16[2,2,1,4,196,768]{5,4,3,2,1,0:T(8,128)(2,1)} %copy.23.pix_ref), custom_call_target="tpu_custom_call" | custom-call | tf_op jit(solution)/shard_map/pick/pallas_call | solution.py:284
  24.5 53.8 %gather.1 = (bf16[32,272,512]{2,1,0:T(8,128)(2,1)}, bf16[2,4,208,768]{3,2,1,0:T(8,128)(2,1)}) custom-call(bf16[272,512]{1,0:T(8,128)(2,1)} %reshape.456.win, bf16[2,4,208,768]{3,2,1,0:T(8,128)(2,1)} %pick.1.pix), custom_call_target="tpu_custom_call" | custom-call | tf_op jit(solution)/shard_map/gather/pallas_call | solution.py:149
  78.3 85.9 %model.1 = (bf16[2,8,16,512]{3,2,1,0:T(8,128)(2,1)}, bf16[8,208,768]{2,1,0:T(8,128)(2,1)}, bf16[8064,512]{1,0:T(8,128)(2,1)}) custom-call(s32[2,4]{1,0:T(2,128)} %get-tuple-element.45.slot_ref, s32[2,4]{1,0:T(2,128)} %get-tuple-element.44.flag_ref, bf16[32,272,512]{2,1,0:T(8,128)(2,1)} %get-tuple-element.10.shards, bf16[8,208,768]{2,1,0:T(8,128)(2,1)} %bitcast.40, ...), custom_call_target="tpu_custom_call" | custom-call | tf_op jit(solution)/shard_map/model/pallas_call | solution.py:883
  164.2 59.5 %reduce.13 = (f32[272,512]{1,0:T(8,128)}, bf16[2,4,208,768]{3,2,1,0:T(8,128)(2,1)}) custom-call(bf16[8064,512]{1,0:T(8,128)(2,1)} %get-tuple-element.13.grads, bf16[2,4,208,768]{3,2,1,0:T(8,128)(2,1)} %bitcast.41), custom_call_target="tpu_custom_call" | custom-call | tf_op jit(solution)/shard_map/reduce/pallas_call | solution.py:249
  223.8 1.2 copy.27
  225.0 1.0 dynamic_slice.3
  226.0 11.1 %place.1 = bf16[2,2,1,4,196,768]{5,4,3,2,1,0:T(8,128)(2,1)} custom-call(s32[2,16]{1,0:T(2,128)} %pad_add_fusion.4.where_ref, bf16[8,208,768]{2,1,0:T(8,128)(2,1)} %bitcast.42), custom_call_target="tpu_custom_call" | custom-call | tf_op jit(solution)/shard_map/place/pallas_call | solution.py:310
  237.1 6.5 %copy.26 = bf16[2,2,1,4,196,768]{5,3,4,2,1,0:T(4,128)(2,1)} copy(bf16[2,2,1,4,196,768]{5,4,3,2,1,0:T(8,128)(2,1)} %place.1) | data formatting | bytes 9633792
  (13 shorter events, 0.1 us)
